TPU v7x, 32 devices: a whole 2x2x4 slice. The times are simulated.
32 devices in a mesh: grp: 2 (over y), chan: 4 (over z), seg: 2 (over x), sub: 2 (over core).
Axes of the slice: x: 2, y: 2, z: 4, core: 2. Of those that a mesh axis runs over, the one named last changes fastest.
Arguments:
- spectra: bfloat16 [8, 64, 2, 1024], P(('grp', 'seg'), 'chan', None, 'sub'), parts along dimension 0, may hold values from -6 to 6
- pair_bin: int32 [4, 4], P('chan'), may hold values from 0 to 3, as said below
Outputs:
- stacks: bfloat16 [8, 16, 16, 128], P(('grp', 'chan'), ('seg', 'sub')), parts along dimension 0
There are 2 independent parts, one for each index of `grp`. A program takes and returns all parts, laid end to end along the dimension named above; an argument that names none is the same for every part. Nothing has to cross between parts.
Inputs may be any that keep to these rules, and one draw needn't show every extreme that they name: In each row of pair_bin one bin, the same for all rows, appears exactly 2 times and every other bin at most once; every bin appears in some row.
All inputs are finite; a program needn't handle non-finite values.
Results may differ from a plain program's by a relative error of at most 0.014.
Values may be sent and summed in bfloat16 or wider, within the bound.
A program may use at most 64 MiB of HBM per device.

v0:
```python
import math

import jax
import jax.numpy as jnp
from jax import lax
from jax.sharding import PartitionSpec as P

FREQ = 1024
LAGS = 128


def from_behind(value, axis, steps):
    count = lax.axis_size(axis)
    pairs = [(source, (source + steps) % count) for source in range(count)]
    return lax.ppermute(value, axis, pairs)


def build_table(band_half, half_width):
    lag_pos = jnp.arange(LAGS, dtype=jnp.int32) - LAGS // 2
    freq_index = band_half * half_width + jnp.arange(half_width, dtype=jnp.int32)
    phases = jnp.mod(freq_index[:, None] * lag_pos[None, :], 2 * FREQ)
    angles = phases.astype(jnp.float32) * (2.0 * math.pi / (2 * FREQ))
    weight = jnp.where(freq_index == 0, 1.0, 2.0).astype(jnp.float32)[:, None]
    return jnp.concatenate([weight * jnp.cos(angles), -weight * jnp.sin(angles)], axis=0).astype(
        jnp.bfloat16
    )


def put_tile(lag_tiles, tile, position):
    return lax.dynamic_update_slice_in_dim(lag_tiles, tile, position, 1)


def local(spectra, pair_bin):
    seg_count = lax.axis_size("seg")
    chan_count = lax.axis_size("chan")
    sub_count = lax.axis_size("sub")
    chan_index = lax.axis_index("chan")
    band_half = lax.axis_index("sub")
    seg_dev = spectra.shape[0]
    ch_dev = spectra.shape[1]
    half_width = spectra.shape[3]
    lag_table = build_table(band_half, half_width)
    norm_scale = 1.0 / math.sqrt(seg_dev * seg_count * half_width * sub_count)
    own_re = spectra[:, :, 0, :]
    own_im = spectra[:, :, 1, :]
    own_parts = jnp.stack(
        [jnp.concatenate([own_re, own_im], axis=0), jnp.concatenate([own_im, -own_re], axis=0)],
        axis=0,
    )
    off_diag = 1.0 - jnp.eye(ch_dev, dtype=jnp.float32)
    all_ones = jnp.ones((ch_dev, ch_dev), jnp.float32)

    def pair_tile(partner, self_mask):
        partner_parts = jnp.concatenate([partner[:, :, 0, :], partner[:, :, 1, :]], axis=0)
        cross_spec = jnp.einsum(
            "pkif,kjf->ijpf", own_parts, partner_parts, preferred_element_type=jnp.float32
        )
        cross_spec = cross_spec * self_mask[:, :, None, None]
        flat_cross = cross_spec.astype(jnp.bfloat16).reshape(ch_dev * ch_dev, 2 * half_width)
        lagged = jnp.dot(flat_cross, lag_table, preferred_element_type=jnp.float32) * norm_scale
        return lagged.reshape(ch_dev, 1, ch_dev, LAGS)

    lag_tiles = jnp.zeros((ch_dev, chan_count, ch_dev, LAGS), jnp.float32)
    lag_tiles = put_tile(lag_tiles, pair_tile(spectra, off_diag), 0)

    def advance(position, carry):
        partner, tiles_now = carry
        partner = from_behind(partner, "chan", 1)
        return (partner, put_tile(tiles_now, pair_tile(partner, all_ones), position))

    partner_last, lag_tiles = lax.fori_loop(1, chan_count, advance, (spectra, lag_tiles))
    own_rows = lax.psum_scatter(
        lag_tiles.astype(jnp.bfloat16), ("seg", "sub"), scatter_dimension=0, tiled=True
    ).astype(jnp.float32)
    step_ids = jnp.arange(chan_count, dtype=jnp.int32)
    partner_ids = jnp.mod(chan_index - step_ids, chan_count)
    bin_row = pair_bin[0]
    step_bin = jnp.sum(
        jnp.where(step_ids[None, :] == partner_ids[:, None], bin_row[None, :], 0), axis=1
    )
    bin_match = step_ids[:, None] == step_bin[None, :]
    bin_load = jnp.sum(bin_match.astype(jnp.float32), axis=1)
    capacity = min(4, chan_count // 2)
    earlier = (step_ids[None, :] < step_ids[:, None]) & (step_bin[None, :] == step_bin[:, None])
    slot_rank = jnp.sum(earlier.astype(jnp.int32), axis=1)
    slot_ids = jnp.arange(capacity, dtype=jnp.int32)
    slot_match = bin_match[:, None, :] & (slot_ids[None, :, None] == slot_rank[None, None, :])
    slot_source = jnp.sum(jnp.where(slot_match, step_ids[None, None, :], 0), axis=2)
    slot_valid = jnp.any(slot_match, axis=2).astype(jnp.float32)
    picked = jnp.take(own_rows, slot_source.reshape(-1), axis=1)
    picked = (
        picked.reshape(own_rows.shape[0], chan_count, capacity, ch_dev, LAGS)
        * slot_valid[None, :, :, None, None]
    )
    incoming, load_in = (
        lax.all_to_all(
            picked.astype(jnp.bfloat16), "chan", split_axis=1, concat_axis=1, tiled=True
        ).astype(picked.dtype),
        lax.all_to_all(
            bin_load[None, :].astype(jnp.bfloat16), "chan", split_axis=1, concat_axis=1, tiled=True
        ).astype(jnp.float32),
    )
    bin_total = jnp.sum(incoming, axis=(1, 2))
    bin_count = jnp.sum(load_in)
    return (bin_total / jnp.sqrt(bin_count))[None].astype(jnp.bfloat16)


def solution(mesh):
    placed = (P(("grp", "seg"), "chan", None, "sub"), P("chan", None))
    return jax.shard_map(
        local,
        mesh=mesh,
        in_specs=placed,
        out_specs=P(("grp", "chan"), ("seg", "sub"), None, None),
        check_vma=False,
    )
```

profile of v0, /device:TPU:0, one launch (start us, length us, event | category | flops | bytes accessed | tf_op | source)
XLA Modules:
  0.0 119.7 jit_solution(7262818912351255018)
XLA Ops:
  6.5 0.8 copy.45
  7.5 0.7 copy.42
  8.2 0.3 copy.51
  8.5 4.0 %fusion.13 = f32[512,16,2,16]{3,1,2,0:T(8,128)} fusion(bf16[4,16,512,1]{1,0,3,2:T(4,128)(2,1)S(1)} %copy.51, bf16[2,4,16,512]{2,1,0,3:T(4,128)(2,1)S(1)} %copy.42), kind=kOutput, calls=%fused_computation.62 | convolution fusion | flops 2097152 | bytes 1245184 | tf_op jit(solution)/shard_map/pkif,kjf->ijpf/dot_general | solution.py:55
  12.5 5.4 %copy.43 = f32[512,16,2,16]{0,1,2,3:T(8,128)S(1)} copy(f32[512,16,2,16]{3,1,2,0:T(8,128)} %fusion.13) | data formatting | bytes 2097152 | tf_op jit(solution)/shard_map/pkif,kjf->ijpf/dot_general | solution.py:55
  18.1 0.5 copy.44
  18.7 1.3 %multiply_convert_fusion.2 = (bf16[512,128]{1,0:T(8,128)(2,1)S(1)}, bf16[512,128]{1,0:T(8,128)(2,1)S(1)}) fusion(s32[128]{0:T(128)S(1)} %iota_add_fusion.1, s32[512]{0:T(512)S(1)} %iota_add_fusion, f32[512]{0:T(512)S(1)} %get-tuple-element.182, f32[512]{0:T(512)S(1)} %get-tuple-element.183), kind=kLoop, calls=%fused_computation.22 | loop fusion | flops 1179648 | bytes 268800 | tf_op jit(solution)/shard_map/convert
  20.4 47.8 %while.17 = (s32[]{:T(128)}, bf16[2,16,2,512]{3,1,0,2:T(8,128)(2,1)S(1)}, bf16[16,4,16,128]{3,2,0,1:T(8,128)(2,1)S(1)}, bf16[2,4,16,512]{2,1,0,3:T(4,128)(2,1)S(...) while((s32[]{:T(128)}, bf16[2,16,2,512]{3,1,0,2:T(8,128)(2,1)S(1)}, ...), condition=%wide.region_4.5_spmd, body=%wide.region_3.4_spmd.sunk | while | flops 69566464 | bytes 4587691 | solution.py:71
  20.4 3.1 %collective-permute-start = (bf16[2,16,2,512]{3,1,0,2:T(8,128)(2,1)S(1)}, bf16[2,16,2,512]{3,1,0,2:T(8,128)(2,1)S(1)}, u32[]{:S(2)}, u32[]{:S(2)}) collective-permute-start(bf16[2,16,2,512]{3,1,0,2:T(8,128)(2,1)S(1)} %get-tuple-element.228), channel_id=1, source_target_pairs={{0,4},{4,8},{8,12},{12,0},{1,5},{5,9},{9,13},{13,1},{2,6},{6,10},{... | collective-permute-start | bytes 196616 | tf_op jit(solution)/shard_map/while/body/eval_jaxpr/ppermute | solution.py:15
  23.5 4.3 %collective-permute-done = bf16[2,16,2,512]{3,1,0,2:T(8,128)(2,1)S(1)} collective-permute-done((bf16[2,16,2,512]{3,1,0,2:T(8,128)(2,1)S(1)}, bf16[2,16,2,512]{3,1,0,2:T(8,128)(2,1)S(1)}, u32[]{:S(2)}, u32[]{:S(2)}) %collective-permute-start) | collective-permute-done | bytes 65568 | tf_op jit(solution)/shard_map/while/body/eval_jaxpr/ppermute | solution.py:15
  27.8 0.3 copy.63
  28.1 2.9 %convert_bitcast_fusion.3 = bf16[16,16,2,512]{0,1,2,3:T(8,128)(2,1)} fusion(bf16[4,16,512,1]{1,0,3,2:T(4,128)(2,1)S(1)} %copy.63, bf16[2,4,16,512]{2,1,0,3:T(4,128)(2,1)S(1)} %get-tuple-element.238), kind=kOutput, calls=%fused_computation.1.clone.1 | convolution fusion | flops 2359296 | bytes 720896 | tf_op jit(solution)/shard_map/while/body/eval_jaxpr/pkif,kjf->ijpf/dot_general | solution.py:55
  31.0 5.8 %copy.64 = bf16[16,16,2,512]{3,2,1,0:T(2,128)(2,1)S(1)} copy(bf16[16,16,2,512]{0,1,2,3:T(8,128)(2,1)} %convert_bitcast_fusion.3) | data formatting | bytes 1048576 | tf_op jit(solution)/shard_map/while/body/eval_jaxpr/convert_element_type | solution.py:59
  37.3 6.0 %collective-permute-done = bf16[2,16,2,512]{3,1,0,2:T(8,128)(2,1)S(1)} collective-permute-done((bf16[2,16,2,512]{3,1,0,2:T(8,128)(2,1)S(1)}, bf16[2,16,2,512]{3,1,0,2:T(8,128)(2,1)S(1)}, u32[]{:S(2)}, u32[]{:S(2)}) %collective-permute-start) | collective-permute-done | bytes 65568 | tf_op jit(solution)/shard_map/while/body/eval_jaxpr/ppermute | solution.py:15
  43.4 0.3 copy.63
  43.7 2.9 %convert_bitcast_fusion.3 = bf16[16,16,2,512]{0,1,2,3:T(8,128)(2,1)} fusion(bf16[4,16,512,1]{1,0,3,2:T(4,128)(2,1)S(1)} %copy.63, bf16[2,4,16,512]{2,1,0,3:T(4,128)(2,1)S(1)} %get-tuple-element.238), kind=kOutput, calls=%fused_computation.1.clone.1 | convolution fusion | flops 2359296 | bytes 720896 | tf_op jit(solution)/shard_map/while/body/eval_jaxpr/pkif,kjf->ijpf/dot_general | solution.py:55
  46.5 5.8 %copy.64 = bf16[16,16,2,512]{3,2,1,0:T(2,128)(2,1)S(1)} copy(bf16[16,16,2,512]{0,1,2,3:T(8,128)(2,1)} %convert_bitcast_fusion.3) | data formatting | bytes 1048576 | tf_op jit(solution)/shard_map/while/body/eval_jaxpr/convert_element_type | solution.py:59
  52.8 6.0 %collective-permute-done = bf16[2,16,2,512]{3,1,0,2:T(8,128)(2,1)S(1)} collective-permute-done((bf16[2,16,2,512]{3,1,0,2:T(8,128)(2,1)S(1)}, bf16[2,16,2,512]{3,1,0,2:T(8,128)(2,1)S(1)}, u32[]{:S(2)}, u32[]{:S(2)}) %collective-permute-start) | collective-permute-done | bytes 65568 | tf_op jit(solution)/shard_map/while/body/eval_jaxpr/ppermute | solution.py:15
  59.2 2.8 %convert_bitcast_fusion.3 = bf16[16,16,2,512]{0,1,2,3:T(8,128)(2,1)} fusion(bf16[4,16,512,1]{1,0,3,2:T(4,128)(2,1)S(1)} %copy.63, bf16[2,4,16,512]{2,1,0,3:T(4,128)(2,1)S(1)} %get-tuple-element.238), kind=kOutput, calls=%fused_computation.1.clone.1 | convolution fusion | flops 2359296 | bytes 720896 | tf_op jit(solution)/shard_map/while/body/eval_jaxpr/pkif,kjf->ijpf/dot_general | solution.py:55
  62.1 5.8 %copy.64 = bf16[16,16,2,512]{3,2,1,0:T(2,128)(2,1)S(1)} copy(bf16[16,16,2,512]{0,1,2,3:T(8,128)(2,1)} %convert_bitcast_fusion.3) | data formatting | bytes 1048576 | tf_op jit(solution)/shard_map/while/body/eval_jaxpr/convert_element_type | solution.py:59
  68.3 0.7 copy-done
  69.3 0.7 copy.49
  70.0 3.2 %all-to-all-start.1 = ((bf16[1,4,1]{2,0,1:T(2,128)(2,1)}), bf16[1,4,1]{2,0,1:T(2,128)(2,1)S(1)}, u32[]{:S(2)}, u32[]{:S(2)}) async-start(bf16[1,4,1]{2,0,1:T(2,128)(2,1)} %copy.49), calls=%async_computation.1 | async-start | bytes 4096 | tf_op jit(solution)/shard_map/all_to_all | solution.py:99
  74.2 0.7 dynamic-slice
  75.6 24.0 %all-reduce.4.cloned.1.call-done = bf16[16,4,16,128]{3,2,0,1:T(8,128)(2,1)} async-done(((bf16[16,4,16,128]{3,2,0,1:T(8,128)(2,1)}), bf16[16,4,16,128]{3,2,0,1:T(8,128)(2,1)}) %all-reduce.4.cloned.1.call-update) | async-done | bytes 262160
  99.6 0.8 dynamic-slice_convert_fusion
  100.4 0.6 gather_fusion
  101.0 0.7 multiply_convert_fusion
  101.7 4.6 %all-to-all-start = ((bf16[4,4,2,16,128]{4,3,0,2,1:T(8,128)(2,1)}), bf16[4,4,2,16,128]{4,3,0,2,1:T(8,128)(2,1)S(1)}, u32[]{:S(2)}, u32[]{:S(2)}) async-start(bf16[4,4,2,16,128]{4,3,0,2,1:T(8,128)(2,1)} %multiply_convert_fusion), calls=%async_computation | async-start | bytes 262144 | tf_op jit(solution)/shard_map/all_to_all | solution.py:96
  106.3 0.6 convert_reduce_fusion.1
  107.6 4.6 %all-to-all-done = bf16[4,4,2,16,128]{4,3,0,2,1:T(8,128)(2,1)S(1)} async-done(((bf16[4,4,2,16,128]{4,3,0,2,1:T(8,128)(2,1)}), bf16[4,4,2,16,128]{4,3,0,2,1:T(8,128)(2,1)S(1)}, u32[]{:S(2)}, u32[]{:S(2)}) %all-to-all-start) | async-done | bytes 131104 | tf_op jit(solution)/shard_map/all_to_all | solution.py:96
  112.3 0.6 fusion.6
  (59 shorter events, 3.5 us)
Async XLA Ops:
  6.5 93.0 %all-reduce.4.cloned.1.call-start = ((), (), s32[]{:S(2)}) async-start(), calls=%async_computation.2 | async-start | bytes 524288
  20.4 48.6 %copy-start.1 = (s32[1,4]{1,0:T(1,128)S(1)}, s32[1,4]{1,0:T(1,128)}, u32[]{:S(2)}) copy-start(s32[1,4]{1,0:T(1,128)} %param.5) | copy-start | bytes 52
  20.4 53.8 %copy-start.2 = (u32[32]{0:T(128)S(1)}, u32[32]{0:T(128)}, u32[]{:S(2)}) copy-start(u32[32]{0:T(128)} %constant.123) | copy-start | bytes 388
  20.4 7.3 %collective-permute-start = (bf16[2,16,2,512]{3,1,0,2:T(8,128)(2,1)S(1)}, bf16[2,16,2,512]{3,1,0,2:T(8,128)(2,1)S(1)}, u32[]{:S(2)}, u32[]{:S(2)}) collective-permute-start(bf16[2,16,2,512]{3,1,0,2:T(8,128)(2,1)S(1)} %get-tuple-element.228), channel_id=1, source_target_pairs={{0,4},{4,8},{8,12},{12,0},{1,5},{5,9},{9,13},{13,1},{2,6},{6,10},{... | collective-permute-start | bytes 196616 | tf_op jit(solution)/shard_map/while/body/eval_jaxpr/ppermute | solution.py:15
  37.2 6.1 %collective-permute-start = (bf16[2,16,2,512]{3,1,0,2:T(8,128)(2,1)S(1)}, bf16[2,16,2,512]{3,1,0,2:T(8,128)(2,1)S(1)}, u32[]{:S(2)}, u32[]{:S(2)}) collective-permute-start(bf16[2,16,2,512]{3,1,0,2:T(8,128)(2,1)S(1)} %get-tuple-element.228), channel_id=1, source_target_pairs={{0,4},{4,8},{8,12},{12,0},{1,5},{5,9},{9,13},{13,1},{2,6},{6,10},{... | collective-permute-start | bytes 196616 | tf_op jit(solution)/shard_map/while/body/eval_jaxpr/ppermute | solution.py:15
  52.8 6.1 %collective-permute-start = (bf16[2,16,2,512]{3,1,0,2:T(8,128)(2,1)S(1)}, bf16[2,16,2,512]{3,1,0,2:T(8,128)(2,1)S(1)}, u32[]{:S(2)}, u32[]{:S(2)}) collective-permute-start(bf16[2,16,2,512]{3,1,0,2:T(8,128)(2,1)S(1)} %get-tuple-element.228), channel_id=1, source_target_pairs={{0,4},{4,8},{8,12},{12,0},{1,5},{5,9},{9,13},{13,1},{2,6},{6,10},{... | collective-permute-start | bytes 196616 | tf_op jit(solution)/shard_map/while/body/eval_jaxpr/ppermute | solution.py:15
  68.3 0.7 copy-start
  70.0 31.7 %all-to-all-start.1 = ((bf16[1,4,1]{2,0,1:T(2,128)(2,1)}), bf16[1,4,1]{2,0,1:T(2,128)(2,1)S(1)}, u32[]{:S(2)}, u32[]{:S(2)}) async-start(bf16[1,4,1]{2,0,1:T(2,128)(2,1)} %copy.49), calls=%async_computation.1 | async-start | bytes 4096 | tf_op jit(solution)/shard_map/all_to_all | solution.py:99
  101.7 10.5 %all-to-all-start = ((bf16[4,4,2,16,128]{4,3,0,2,1:T(8,128)(2,1)}), bf16[4,4,2,16,128]{4,3,0,2,1:T(8,128)(2,1)S(1)}, u32[]{:S(2)}, u32[]{:S(2)}) async-start(bf16[4,4,2,16,128]{4,3,0,2,1:T(8,128)(2,1)} %multiply_convert_fusion), calls=%async_computation | async-start | bytes 262144 | tf_op jit(solution)/shard_map/all_to_all | solution.py:96
Sparse Core Ops, SparseCore 0:
  69.1 30.3 all-reduce.3
where the time goes:
time: 120 us
  waiting for transfers between devices  45 us (38%)
  local copies, waits for them, and re-layouts  29.5 us (25%)
  between operations  15 us (12%)
  matrix products  13.7 us (11%)
  starting transfers between devices  11 us (9%)
  other arithmetic  5.24 us (4%)
    unnamed x2, waiting for transfers between devices  24 us
    convert_element_type x4, local copies, waits for them, and re-layouts, pair_tile(): cross_spec.astype(jnp.bfloat16).reshape(ch_dev * ch_dev, 2 * half_width)  17.9 us
    ppermute x3, waiting for transfers between devices, from_behind(): return lax.ppermute(value, axis, pairs)  16.4 us
    dot_general x4, matrix products, pair_tile(): jnp.einsum('pkif,kjf->ijpf', own_parts, partner_parts, preferred_element_...  12.6 us
    dot_general x1, local copies, waits for them, and re-layouts, pair_tile(): jnp.einsum('pkif,kjf->ijpf', own_parts, partner_parts, preferred_element_...  5.39 us
    all_to_all x1, waiting for transfers between devices, local(): lax.all_to_all(picked.astype(jnp.bfloat16), 'chan', split_axis=1, concat_...  4.62 us
    all_to_all x1, starting transfers between devices, local(): lax.all_to_all(picked.astype(jnp.bfloat16), 'chan', split_axis=1, concat_...  4.6 us
    all_to_all x1, starting transfers between devices, local(): lax.all_to_all(bin_load[None, :].astype(jnp.bfloat16), 'chan', split_axis...  3.22 us
  transfers between devices with their start and end apart: 6, of which 5 were waited for; matrix products, arithmetic and copies ran while one was open for 4% of the time, Pallas kernels for 0%

commit v1 on v0

v1 whole, which is shorter than its diff:
```python
import functools
import math

import jax
import jax.numpy as jnp
import numpy as np
from jax import lax
from jax.experimental import pallas as pl
from jax.experimental.pallas import tpu as pltpu
from jax.sharding import PartitionSpec as P

LAGS = 128
LANES = 128
MESH = pl.DeviceIdType.MESH


def lag_table(sub_count, half_width):
    freq_total = sub_count * half_width
    lag_pos = np.arange(LAGS) - LAGS // 2
    freq = np.arange(freq_total)
    phases = np.mod(freq[:, None] * lag_pos[None, :], 2 * freq_total)
    angles = phases.astype(np.float32) * np.float32(2.0 * math.pi / (2 * freq_total))
    weight = np.where(freq == 0, 1.0, 2.0).astype(np.float32)[:, None]
    parts = np.stack([weight * np.cos(angles), -weight * np.sin(angles)], axis=0)
    parts = parts.reshape(2, sub_count, half_width // LANES, LANES, LAGS)
    parts = parts.transpose(1, 2, 0, 3, 4).reshape(sub_count, -1, 2 * LANES, LAGS)
    return parts.astype(jnp.bfloat16)


def kernel(
    sizes, x_ref, bins_ref, table_hbm, out_ref,
    blocks, bins_all, table, wide, mixed, weights, cross, total, leave, land,
    bins_send, bins_recv, block_send, block_recv, part_send, part_recv, table_sem,
):
    chans, segs, subs, seg_dev, ch, tiles, norm = sizes
    me = lax.axis_index("chan")
    seg_me = lax.axis_index("seg")
    sub_me = lax.axis_index("sub")
    spot = seg_me * subs + sub_me
    spots = segs * subs
    out_rows = ch // spots
    unroll = chans <= 4

    load_table = pltpu.make_async_copy(table_hbm.at[sub_me], table, table_sem)
    load_table.start()

    barrier = pltpu.get_barrier_semaphore()
    for away in range(1, chans):
        pl.semaphore_signal(
            barrier, inc=1, device_id={"chan": lax.rem(me + away, chans)}, device_id_type=MESH
        )
    for away in range(1, spots):
        other = lax.rem(spot + away, spots)
        pl.semaphore_signal(
            barrier, inc=1, device_id={"seg": other // subs, "sub": lax.rem(other, subs)},
            device_id_type=MESH,
        )

    for k in range(seg_dev):
        for part in range(2):
            rows = x_ref[k, :, part, :]
            for tile in range(tiles):
                blocks[me, tile, pl.ds((k * 2 + part) * ch, ch), :] = rows[
                    :, tile * LANES : (tile + 1) * LANES
                ]
    row_ids = lax.broadcasted_iota(jnp.int32, bins_all.shape[1:], 0)
    bin_rows = jnp.full(bins_all.shape[1:], -1, jnp.int32)
    for b in range(chans):
        bin_rows = jnp.where(row_ids == b, bins_ref[0, b], bin_rows)
    bins_all[me] = bin_rows

    pl.semaphore_wait(barrier, chans - 1 + spots - 1)

    def bins_copy(source, target):
        return pltpu.make_async_remote_copy(
            src_ref=bins_all.at[source], dst_ref=bins_all.at[source],
            send_sem=bins_send.at[target], recv_sem=bins_recv.at[source],
            device_id={"chan": target}, device_id_type=MESH,
        )

    def block_copy(source, target, tile):
        return pltpu.make_async_remote_copy(
            src_ref=blocks.at[source, tile], dst_ref=blocks.at[source, tile],
            send_sem=block_send.at[target, tile], recv_sem=block_recv.at[source, tile],
            device_id={"chan": target}, device_id_type=MESH,
        )

    def part_copy(target):
        return pltpu.make_async_remote_copy(
            src_ref=leave.at[target], dst_ref=land.at[spot],
            send_sem=part_send.at[target], recv_sem=part_recv.at[spot],
            device_id={"seg": target // subs, "sub": lax.rem(target, subs)}, device_id_type=MESH,
        )

    def part_arrival(source):
        return pltpu.make_async_remote_copy(
            src_ref=leave.at[source], dst_ref=land.at[source],
            send_sem=part_send.at[source], recv_sem=part_recv.at[source],
            device_id={"seg": source // subs, "sub": lax.rem(source, subs)}, device_id_type=MESH,
        )

    others = [lax.rem(me + away, chans) for away in range(1, chans)]
    for target in others:
        bins_copy(me, target).start()
    for tile in range(tiles):
        for target in others:
            block_copy(me, target, tile).start()

    for source in others:
        bins_copy(source, source).wait_recv()
    match = (bins_all[...] == me).astype(jnp.float32)
    weights[...] = match
    pair_count = jnp.sum(jnp.sum(match, axis=0), axis=0, keepdims=True)
    scale = norm / jnp.sqrt(pair_count)

    j_ids = lax.broadcasted_iota(jnp.int32, (ch, LANES), 0)
    half = seg_dev * 2 * ch

    for tile in range(tiles):
        for source in others:
            block_copy(source, source, tile).wait_recv()

        def widen(a, carry, tile=tile):
            wide[a] = blocks[a, tile].astype(jnp.float32)
            return carry

        lax.fori_loop(0, chans, widen, 0, unroll=unroll)

        def mix(a, carry):
            diag_re, diag_im = carry

            def add(b, sums):
                weight = weights[a, pl.ds(b, 1), :]
                apart = weight * (b != a).astype(jnp.float32)
                return sums[0] + weight * wide[b], sums[1] + apart * wide[b]

            zero = jnp.zeros((half, LANES), jnp.float32)
            full, off = lax.fori_loop(0, chans, add, (zero, zero), unroll=unroll)
            mixed[a] = full
            for k in range(seg_dev):
                re, im = k * 2 * ch, (k * 2 + 1) * ch
                x_re, x_im = wide[a, pl.ds(re, ch), :], wide[a, pl.ds(im, ch), :]
                y_re, y_im = off[re : re + ch], off[im : im + ch]
                diag_re = diag_re + (x_re * y_re + x_im * y_im)
                diag_im = diag_im + (x_im * y_re - x_re * y_im)
            return diag_re, diag_im

        zero = jnp.zeros((ch, LANES), jnp.float32)
        diag_re, diag_im = lax.fori_loop(0, chans, mix, (zero, zero), unroll=unroll)

        def rows_of(group, carry):
            first = group * out_rows

            def add(a, sums):
                sums = list(sums)
                for k in range(seg_dev):
                    re, im = k * 2 * ch, (k * 2 + 1) * ch
                    y_re, y_im = mixed[a, pl.ds(re, ch), :], mixed[a, pl.ds(im, ch), :]
                    for r in range(out_rows):
                        x_re = wide[a, pl.ds(re + first + r, 1), :]
                        x_im = wide[a, pl.ds(im + first + r, 1), :]
                        sums[2 * r] = sums[2 * r] + (x_re * y_re + x_im * y_im)
                        sums[2 * r + 1] = sums[2 * r + 1] + (x_im * y_re - x_re * y_im)
                return tuple(sums)

            start = tuple(jnp.zeros((ch, LANES), jnp.float32) for _ in range(2 * out_rows))
            sums = lax.fori_loop(0, chans, add, start, unroll=unroll)
            for r in range(out_rows):
                on_diag = j_ids == first + r
                at = pl.ds(pl.multiple_of((first + r) * ch, ch), ch)
                cross[at, :LANES] = jnp.where(on_diag, diag_re, sums[2 * r]).astype(jnp.bfloat16)
                cross[at, LANES:] = jnp.where(on_diag, diag_im, sums[2 * r + 1]).astype(jnp.bfloat16)
            return carry

        lax.fori_loop(0, spots, rows_of, 0)
        if tile == 0:
            load_table.wait()
        lags = jnp.dot(cross[...], table[tile], preferred_element_type=jnp.float32)
        if tile == 0:
            total[...] = lags
        else:
            total[...] += lags

    depth = out_rows * ch
    near = [lax.rem(spot + away, spots) for away in range(1, spots)]
    for target in near:
        at = pl.ds(pl.multiple_of(target * depth, depth), depth)
        leave[target] = (total[at, :] * norm).astype(jnp.bfloat16)
        part_copy(target).start()
    own = total[pl.ds(pl.multiple_of(spot * depth, depth), depth), :] * norm
    for source in near:
        part_arrival(source).wait_recv()
        own = own + land[source].astype(jnp.float32)
    own = own * (scale / norm)
    for r in range(out_rows):
        out_ref[0, r] = own[r * ch : (r + 1) * ch].astype(jnp.bfloat16)

    for target in others:
        bins_copy(me, target).wait_send()
        for tile in range(tiles):
            block_copy(me, target, tile).wait_send()
    for target in near:
        part_copy(target).wait_send()


def local(table_all, spectra, pair_bin):
    segs, chans, subs = lax.axis_size("seg"), lax.axis_size("chan"), lax.axis_size("sub")
    seg_dev, ch, _, half_width = spectra.shape
    tiles = half_width // LANES
    spots = segs * subs
    out_rows = ch // spots
    norm = 1.0 / math.sqrt(seg_dev * segs * half_width * subs)
    rows = seg_dev * 2 * ch
    padded = -(-chans // 8) * 8
    sizes = (chans, segs, subs, seg_dev, ch, tiles, norm)
    dma = pltpu.SemaphoreType.DMA
    return pl.pallas_call(
        functools.partial(kernel, sizes),
        out_shape=jax.ShapeDtypeStruct((1, out_rows, ch, LAGS), jnp.bfloat16),
        in_specs=[
            pl.BlockSpec(memory_space=pltpu.VMEM),
            pl.BlockSpec(memory_space=pltpu.SMEM),
            pl.BlockSpec(memory_space=pl.ANY),
        ],
        out_specs=pl.BlockSpec(memory_space=pltpu.VMEM),
        scratch_shapes=[
            pltpu.VMEM((chans, tiles, rows, LANES), jnp.bfloat16),
            pltpu.VMEM((chans, padded, LANES), jnp.int32),
            pltpu.VMEM((tiles, 2 * LANES, LAGS), jnp.bfloat16),
            pltpu.VMEM((chans, rows, LANES), jnp.float32),
            pltpu.VMEM((chans, rows, LANES), jnp.float32),
            pltpu.VMEM((chans, padded, LANES), jnp.float32),
            pltpu.VMEM((ch * ch, 2 * LANES), jnp.bfloat16),
            pltpu.VMEM((ch * ch, LAGS), jnp.float32),
            pltpu.VMEM((spots, out_rows * ch, LAGS), jnp.bfloat16),
            pltpu.VMEM((spots, out_rows * ch, LAGS), jnp.bfloat16),
            dma((chans,)),
            dma((chans,)),
            dma((chans, tiles)),
            dma((chans, tiles)),
            dma((spots,)),
            dma((spots,)),
            dma,
        ],
        compiler_params=pltpu.CompilerParams(
            collective_id=0, has_side_effects=True, vmem_limit_bytes=32 * 2**20
        ),
    )(spectra, pair_bin, table_all)


def solution(mesh):
    sub_count = mesh.shape["sub"]

    def run(spectra, pair_bin):
        half_width = spectra.shape[3] // sub_count
        table_all = jnp.asarray(lag_table(sub_count, half_width))
        placed = (P(), P(("grp", "seg"), "chan", None, "sub"), P("chan", None))
        return jax.shard_map(
            local,
            mesh=mesh,
            in_specs=placed,
            out_specs=P(("grp", "chan"), ("seg", "sub"), None, None),
            check_vma=False,
        )(table_all, spectra, pair_bin)

    return run
```

time: 120 us -> 20.4 us (0.17)
  waiting for transfers between devices: 45 us -> 0 us
  local copies, waits for them, and re-layouts: 29.5 us -> 3.14 us
  Pallas kernels: 0 us -> 17 us
  between operations: 15 us -> 0.01 us
  matrix products: 13.7 us -> 0 us
  starting transfers between devices: 11 us -> 0 us
  other arithmetic: 5.24 us -> 0 us
    unnamed x2 -> x0, waiting for transfers between devices: 24 us -> none
    convert_element_type x6 -> x0, local copies, waits for them, and re-layouts: 18.7 us -> none  [the longest x4 17.9 us: pair_tile(): cross_spec.astype(jnp.bfloat16).reshape(ch_dev * ch_dev, 2 * half_width)]
    pallas_call x0 -> x1, Pallas kernels: none -> 17 us  [local(): pl.pallas_call(functools.partial(kernel, sizes), out_shape=jax.ShapeDtype...]
    ppermute x3 -> x0, waiting for transfers between devices: 16.4 us -> none  [from_behind(): return lax.ppermute(value, axis, pairs)]
    dot_general x8 -> x0, matrix products: 13.7 us -> none  [the longest x4 12.6 us: pair_tile(): jnp.einsum('pkif,kjf->ijpf', own_parts, partner_parts, preferred_element_...]
    all_to_all x2 -> x0, starting transfers between devices: 7.82 us -> none  [the longest x1 4.6 us: local(): lax.all_to_all(picked.astype(jnp.bfloat16), 'chan', split_axis=1, concat_...]
    dot_general x1 -> x0, local copies, waits for them, and re-layouts: 5.39 us -> none  [pair_tile(): jnp.einsum('pkif,kjf->ijpf', own_parts, partner_parts, preferred_element_...]
    all_to_all x2 -> x0, waiting for transfers between devices: 4.63 us -> none  [the longest x1 4.62 us: local(): lax.all_to_all(picked.astype(jnp.bfloat16), 'chan', split_axis=1, concat_...]
  transfers between devices with their start and end apart: 6 -> 0, of which waited for: 5 -> 0; matrix products, arithmetic and copies ran while one was open for 4% -> 0% of each run, Pallas kernels for 0% -> 0%
where the time goes in v1:
time: 20.4 us; the launch traced here: 20.2 us
  Pallas kernels  17 us (83%)
  local copies, waits for them, and re-layouts  3.14 us (15%)
    pallas_call x1, Pallas kernels, local(): pl.pallas_call(functools.partial(kernel, sizes), out_shape=jax.ShapeDtype...  17 us
    unnamed x7, local copies, waits for them, and re-layouts  3.14 us

profile of v1, /device:TPU:0, one launch (start us, length us, event | category | flops | bytes accessed | tf_op | source)
XLA Modules:
  0.0 20.2 jit_solution(4324439402020510847)
XLA Ops:
  0.0 0.0 copy-start
  0.0 1.0 %copy-done = bf16[2,4,256,128]{3,2,1,0:T(8,128)(2,1)S(1)} copy-done((bf16[2,4,256,128]{3,2,1,0:T(8,128)(2,1)S(1)}, bf16[2,4,256,128]{3,2,1,0:T(8,128)(2,1)}, u32[]{:S(2)}) %copy-start) | copy-done | bytes 524312
  1.0 0.0 copy-start.1
  1.0 0.8 %copy-done.1 = bf16[2,16,2,512]{3,2,1,0:T(2,128)(2,1)S(1)} copy-done((bf16[2,16,2,512]{3,2,1,0:T(2,128)(2,1)S(1)}, bf16[2,16,2,512]{3,2,1,0:T(2,128)(2,1)}, u32[]{:S(2)}) %copy-start.1) | copy-done | bytes 65560
  1.9 0.0 copy-start.2
  1.9 0.7 %copy-done.2 = s32[1,4]{1,0:T(1,128)S(1)} copy-done((s32[1,4]{1,0:T(1,128)S(1)}, s32[1,4]{1,0:T(1,128)}, u32[]{:S(2)}) %copy-start.2) | copy-done | bytes 40
  2.5 17.0 %shard_map.37 = bf16[1,4,16,128]{3,2,1,0:T(8,128)(2,1)S(1)} custom-call(bf16[2,16,2,512]{3,2,1,0:T(2,128)(2,1)S(1)} %copy-done.1, s32[1,4]{1,0:T(1,128)S(1)} %copy-done.2, bf16[2,4,256,128]{3,2,1,0:T(8,128)(2,1)S(1)} %copy-done), custom_call_target="tpu_custom_call" | custom-call | tf_op jit(solution)/shard_map/pallas_call | solution.py:217
  19.6 0.6 %copy.5 = bf16[1,4,16,128]{3,2,1,0:T(8,128)(2,1)} copy(bf16[1,4,16,128]{3,2,1,0:T(8,128)(2,1)S(1)} %shard_map.37) | data formatting | bytes 32768
Async XLA Ops:
  0.0 1.0 %copy-start = (bf16[2,4,256,128]{3,2,1,0:T(8,128)(2,1)S(1)}, bf16[2,4,256,128]{3,2,1,0:T(8,128)(2,1)}, u32[]{:S(2)}) copy-start(bf16[2,4,256,128]{3,2,1,0:T(8,128)(2,1)} %constant.2.clone.table_hbm) | copy-start | bytes 1572868
  1.0 0.8 %copy-start.1 = (bf16[2,16,2,512]{3,2,1,0:T(2,128)(2,1)S(1)}, bf16[2,16,2,512]{3,2,1,0:T(2,128)(2,1)}, u32[]{:S(2)}) copy-start(bf16[2,16,2,512]{3,2,1,0:T(2,128)(2,1)} %x_ref.1) | copy-start | bytes 196612
  1.9 0.7 %copy-start.2 = (s32[1,4]{1,0:T(1,128)S(1)}, s32[1,4]{1,0:T(1,128)}, u32[]{:S(2)}) copy-start(s32[1,4]{1,0:T(1,128)} %bins_ref.1) | copy-start | bytes 52

commit v2 on v1

v2 whole, which is shorter than its diff:
```python
import functools
import math

import jax
import jax.numpy as jnp
import numpy as np
from jax import lax
from jax.experimental import pallas as pl
from jax.experimental.pallas import tpu as pltpu
from jax.sharding import PartitionSpec as P

LAGS = 128
LANES = 128
MESH = pl.DeviceIdType.MESH


def lag_table(sub_count, half_width):
    freq_total = sub_count * half_width
    lag_pos = np.arange(LAGS) - LAGS // 2
    freq = np.arange(freq_total)
    phases = np.mod(freq[:, None] * lag_pos[None, :], 2 * freq_total)
    angles = phases.astype(np.float32) * np.float32(2.0 * math.pi / (2 * freq_total))
    weight = np.where(freq == 0, 1.0, 2.0).astype(np.float32)[:, None]
    parts = np.stack([weight * np.cos(angles), -weight * np.sin(angles)], axis=0)
    parts = parts.reshape(2, sub_count, half_width // LANES, LANES, LAGS)
    parts = parts.transpose(1, 2, 0, 3, 4).reshape(sub_count, -1, 2 * LANES, LAGS)
    return parts.astype(jnp.bfloat16)


def kernel(
    sizes, x_hbm, bins_hbm, table_hbm, out_ref,
    raw, bins_all, table, wide, mixed, weights, cross, total, leave, land,
    bins_send, bins_recv, block_send, block_recv, part_send, part_recv, load_sem,
):
    chans, pair, segs, subs, seg_dev, ch, tiles, norm = sizes
    me = lax.axis_index("chan")
    spot = lax.axis_index("seg") * subs + lax.axis_index("sub")
    spots = segs * subs
    out_rows = ch // spots
    depth = out_rows * ch
    unroll = chans <= 4
    side = lax.rem(me, pair)
    base = me - side
    others = [lax.rem(me + away, chans) for away in range(1, chans)]
    near = [lax.rem(spot + away, spots) for away in range(1, spots)]

    def device(member, place):
        return {"chan": base + member, "seg": place // subs, "sub": lax.rem(place, subs)}

    barrier = pltpu.get_barrier_semaphore()
    for target in others:
        pl.semaphore_signal(barrier, inc=1, device_id={"chan": target}, device_id_type=MESH)
    for member in range(pair):
        for place in near:
            pl.semaphore_signal(
                barrier, inc=1, device_id=device(member, place), device_id_type=MESH
            )

    def lanes_of(target, tile):
        start = (lax.rem(target, pair) * tiles + tile) * LANES
        return x_hbm.at[:, :, :, pl.ds(pl.multiple_of(start, LANES), LANES)]

    own_tiles = [
        pltpu.make_async_copy(lanes_of(me, tile), raw.at[me, tile], load_sem.at[2 + tile])
        for tile in range(tiles)
    ]
    load_bins = pltpu.make_async_copy(bins_hbm, bins_all.at[me], load_sem.at[0])
    load_table = pltpu.make_async_copy(
        table_hbm.at[lax.axis_index("sub"), pl.ds(side * tiles, tiles)], table, load_sem.at[1]
    )
    load_bins.start()
    for own_tile in own_tiles:
        own_tile.start()
    load_table.start()

    pl.semaphore_wait(barrier, chans - 1 + pair * (spots - 1))

    def bins_copy(source, target):
        return pltpu.make_async_remote_copy(
            src_ref=bins_hbm, dst_ref=bins_all.at[source],
            send_sem=bins_send.at[target], recv_sem=bins_recv.at[source],
            device_id={"chan": target}, device_id_type=MESH,
        )

    def block_copy(source, target, tile):
        return pltpu.make_async_remote_copy(
            src_ref=lanes_of(target, tile), dst_ref=raw.at[source, tile],
            send_sem=block_send.at[target, tile], recv_sem=block_recv.at[source, tile],
            device_id={"chan": target}, device_id_type=MESH,
        )

    def part_copy(member, place, from_member, from_place):
        return pltpu.make_async_remote_copy(
            src_ref=leave.at[member, place], dst_ref=land.at[from_member, from_place],
            send_sem=part_send.at[member, place], recv_sem=part_recv.at[from_member, from_place],
            device_id=device(member, place), device_id_type=MESH,
        )

    for target in others:
        bins_copy(me, target).start()
    for tile in range(tiles):
        for target in others:
            block_copy(me, target, tile).start()

    load_bins.wait()
    for source in others:
        bins_copy(source, source).wait_recv()
    padded = weights.shape[2]
    row_ids = lax.broadcasted_iota(jnp.int32, (padded, chans), 0)
    col_ids = lax.broadcasted_iota(jnp.int32, (padded, chans), 1)
    wide_ids = lax.broadcasted_iota(jnp.int32, (padded, LANES), 0)

    def weigh(a, carry):
        row = jnp.broadcast_to(bins_all[a].astype(jnp.float32), (padded, chans))
        column = jnp.sum(jnp.where(row_ids == col_ids, row, 0.0), axis=1, keepdims=True)
        column = jnp.where(wide_ids < chans, jnp.broadcast_to(column, (padded, LANES)), -1.0)
        for member in range(pair):
            weights[member, a] = (column == (base + member).astype(jnp.float32)).astype(jnp.float32)
        return carry

    lax.fori_loop(0, chans, weigh, 0, unroll=unroll)
    pair_count = jnp.sum(jnp.sum(weights[side], axis=0), axis=0, keepdims=True)
    scale = 1.0 / jnp.sqrt(pair_count)

    j_ids = lax.broadcasted_iota(jnp.int32, (ch, LANES), 0)
    rows = seg_dev * 2 * ch

    for tile in range(tiles):
        own_tiles[tile].wait()
        for source in others:
            block_copy(source, me, tile).wait_recv()

        def widen(a, carry, tile=tile):
            for k in range(seg_dev):
                for part in range(2):
                    at = pl.ds((k * 2 + part) * ch, ch)
                    wide[a, at, :] = raw[a, tile, k, :, part, :].astype(jnp.float32)
            return carry

        lax.fori_loop(0, chans, widen, 0, unroll=unroll)

        for step in range(pair):
            member = lax.rem(side + 1 + step, pair)

            def mix(a, carry, member=member):
                diag_re, diag_im = carry

                def add(b, sums):
                    weight = weights[member, a, pl.ds(b, 1), :]
                    apart = weight * jnp.not_equal(b, a).astype(jnp.float32)
                    return sums[0] + weight * wide[b], sums[1] + apart * wide[b]

                zero = jnp.zeros((rows, LANES), jnp.float32)
                full, off = lax.fori_loop(0, chans, add, (zero, zero), unroll=unroll)
                mixed[a] = full
                for k in range(seg_dev):
                    re, im = k * 2 * ch, (k * 2 + 1) * ch
                    x_re, x_im = wide[a, pl.ds(re, ch), :], wide[a, pl.ds(im, ch), :]
                    y_re, y_im = off[re : re + ch], off[im : im + ch]
                    diag_re = diag_re + (x_re * y_re + x_im * y_im)
                    diag_im = diag_im + (x_im * y_re - x_re * y_im)
                return diag_re, diag_im

            zero = jnp.zeros((ch, LANES), jnp.float32)
            diag_re, diag_im = lax.fori_loop(0, chans, mix, (zero, zero), unroll=unroll)

            def rows_of(group, carry, diag_re=diag_re, diag_im=diag_im):
                first = group * out_rows

                def add(a, sums):
                    sums = list(sums)
                    for k in range(seg_dev):
                        re, im = k * 2 * ch, (k * 2 + 1) * ch
                        y_re, y_im = mixed[a, pl.ds(re, ch), :], mixed[a, pl.ds(im, ch), :]
                        for r in range(out_rows):
                            x_re = wide[a, pl.ds(re + first + r, 1), :]
                            x_im = wide[a, pl.ds(im + first + r, 1), :]
                            sums[2 * r] = sums[2 * r] + (x_re * y_re + x_im * y_im)
                            sums[2 * r + 1] = sums[2 * r + 1] + (x_im * y_re - x_re * y_im)
                    return tuple(sums)

                start = tuple(jnp.zeros((ch, LANES), jnp.float32) for _ in range(2 * out_rows))
                sums = lax.fori_loop(0, chans, add, start, unroll=unroll)
                for r in range(out_rows):
                    diag = j_ids == first + r
                    at = pl.ds(pl.multiple_of((first + r) * ch, ch), ch)
                    cross[at, :LANES] = jnp.where(diag, diag_re, sums[2 * r]).astype(jnp.bfloat16)
                    cross[at, LANES:] = jnp.where(diag, diag_im, sums[2 * r + 1]).astype(
                        jnp.bfloat16
                    )
                return carry

            lax.fori_loop(0, spots, rows_of, 0)
            if tile == 0 and step == 0:
                load_table.wait()
            lags = jnp.dot(cross[...], table[tile], preferred_element_type=jnp.float32)
            if tile > 0:
                lags = lags + total[member]
            if tile < tiles - 1:
                total[member] = lags
                continue
            lags = lags * norm
            for place in range(spots):
                leave[member, place] = lags[place * depth : (place + 1) * depth].astype(jnp.bfloat16)
            if step < pair - 1:
                part_copy(member, spot, side, spot).start()
            else:
                total[member] = lags
            for place in near:
                part_copy(member, place, side, spot).start()

    own = total[side, pl.ds(pl.multiple_of(spot * depth, depth), depth), :]
    for step in range(pair):
        member = lax.rem(side + 1 + step, pair)
        for place in near + [spot] * (step < pair - 1):
            part_copy(member, place, member, place).wait_recv()
            own = own + land[member, place].astype(jnp.float32)
    own = own * scale
    for r in range(out_rows):
        out_ref[0, r] = own[r * ch : (r + 1) * ch].astype(jnp.bfloat16)

    for target in others:
        bins_copy(me, target).wait_send()
        for tile in range(tiles):
            block_copy(me, target, tile).wait_send()
    for step in range(pair):
        member = lax.rem(side + 1 + step, pair)
        for place in near + [spot] * (step < pair - 1):
            part_copy(member, place, side, spot).wait_send()


def local(table_all, spectra, pair_bin):
    segs, chans, subs = lax.axis_size("seg"), lax.axis_size("chan"), lax.axis_size("sub")
    seg_dev, ch, _, half_width = spectra.shape
    pair = 2 if chans % 2 == 0 else 1
    tiles = half_width // LANES // pair
    spots = segs * subs
    out_rows = ch // spots
    norm = 1.0 / math.sqrt(seg_dev * segs * half_width * subs)
    rows = seg_dev * 2 * ch
    padded = -(-chans // 8) * 8
    sizes = (chans, pair, segs, subs, seg_dev, ch, tiles, norm)
    dma = pltpu.SemaphoreType.DMA
    in_hbm = pl.BlockSpec(memory_space=pl.ANY)
    return pl.pallas_call(
        functools.partial(kernel, sizes),
        out_shape=pltpu.VMEM((1, out_rows, ch, LAGS), jnp.bfloat16),
        in_specs=[in_hbm, in_hbm, in_hbm],
        out_specs=pl.BlockSpec(memory_space=pltpu.VMEM),
        scratch_shapes=[
            pltpu.VMEM((chans, tiles, seg_dev, ch, 2, LANES), jnp.bfloat16),
            pltpu.VMEM((chans, 1, chans), jnp.int32),
            pltpu.VMEM((tiles, 2 * LANES, LAGS), jnp.bfloat16),
            pltpu.VMEM((chans, rows, LANES), jnp.float32),
            pltpu.VMEM((chans, rows, LANES), jnp.float32),
            pltpu.VMEM((pair, chans, padded, LANES), jnp.float32),
            pltpu.VMEM((ch * ch, 2 * LANES), jnp.bfloat16),
            pltpu.VMEM((pair, ch * ch, LAGS), jnp.float32),
            pltpu.VMEM((pair, spots, out_rows * ch, LAGS), jnp.bfloat16),
            pltpu.VMEM((pair, spots, out_rows * ch, LAGS), jnp.bfloat16),
            dma((chans,)),
            dma((chans,)),
            dma((chans, tiles)),
            dma((chans, tiles)),
            dma((pair, spots)),
            dma((pair, spots)),
            dma((2 + tiles,)),
        ],
        compiler_params=pltpu.CompilerParams(
            collective_id=0, has_side_effects=True, vmem_limit_bytes=60 * 2**20
        ),
    )(spectra, pair_bin, table_all)


def solution(mesh):
    sub_count = mesh.shape["sub"]

    def run(spectra, pair_bin):
        half_width = spectra.shape[3] // sub_count
        table_all = jnp.asarray(lag_table(sub_count, half_width))
        placed = (P(), P(("grp", "seg"), "chan", None, "sub"), P("chan", None))
        return jax.shard_map(
            local,
            mesh=mesh,
            in_specs=placed,
            out_specs=P(("grp", "chan"), ("seg", "sub"), None, None),
            check_vma=False,
        )(table_all, spectra, pair_bin)

    return run
```

time: 20.4 us -> 16 us (0.78)
  local copies, waits for them, and re-layouts: 3.14 us -> 0.61 us
  Pallas kernels: 17 us -> 15.2 us
    unnamed x7 -> x1, local copies, waits for them, and re-layouts: 3.14 us -> 0.61 us
    pallas_call x1, Pallas kernels: 17 us -> 15.2 us  [local(): pl.pallas_call(functools.partial(kernel, sizes), out_shape=pltpu.VMEM((1,...]
where the time goes in v2:
time: 16 us; the launch traced here: 15.8 us
  Pallas kernels  15.2 us (95%)
  local copies, waits for them, and re-layouts  0.61 us (4%)
    pallas_call x1, Pallas kernels, local(): pl.pallas_call(functools.partial(kernel, sizes), out_shape=pltpu.VMEM((1,...  15.2 us
    unnamed x1, local copies, waits for them, and re-layouts  0.61 us

profile of v2, /device:TPU:0, one launch (start us, length us, event | category | flops | bytes accessed | tf_op | source)
XLA Modules:
  0.0 15.8 jit_solution(18274530542830043508)
XLA Ops:
  0.0 15.2 %shard_map.37 = bf16[1,4,16,128]{3,2,1,0:T(8,128)(2,1)S(1)} custom-call(bf16[2,16,2,512]{3,2,1,0:T(2,128)(2,1)} %x_hbm.1, s32[1,4]{1,0:T(1,128)} %bins_hbm.1, bf16[2,4,256,128]{3,2,1,0:T(8,128)(2,1)} %constant.2.clone.table_hbm), custom_call_target="tpu_custom_call" | custom-call | tf_op jit(solution)/shard_map/pallas_call | solution.py:245
  15.2 0.6 %copy.5 = bf16[1,4,16,128]{3,2,1,0:T(8,128)(2,1)} copy(bf16[1,4,16,128]{3,2,1,0:T(8,128)(2,1)S(1)} %shard_map.37) | data formatting | bytes 32768

commit v3 on v2

--- a/solution.py
+++ b/solution.py
@@ -29,7 +29,7 @@
 
 def kernel(
     sizes, x_hbm, bins_hbm, table_hbm, out_ref,
-    raw, bins_all, table, wide, mixed, weights, cross, total, leave, land,
+    own, raw, bins_all, table, wide, mixed, weights, total, leave, land,
     bins_send, bins_recv, block_send, block_recv, part_send, part_recv, load_sem,
 ):
     chans, pair, segs, subs, seg_dev, ch, tiles, norm = sizes
@@ -37,12 +37,15 @@
     spot = lax.axis_index("seg") * subs + lax.axis_index("sub")
     spots = segs * subs
     out_rows = ch // spots
-    depth = out_rows * ch
     unroll = chans <= 4
     side = lax.rem(me, pair)
     base = me - side
     others = [lax.rem(me + away, chans) for away in range(1, chans)]
-    near = [lax.rem(spot + away, spots) for away in range(1, spots)]
+    aways = list(range(subs, spots)) + list(range(1, subs))
+    near = [
+        lax.rem(spot // subs + away // subs, segs) * subs + lax.rem(spot + away, subs)
+        for away in aways
+    ]
 
     def device(member, place):
         return {"chan": base + member, "seg": place // subs, "sub": lax.rem(place, subs)}
@@ -56,35 +59,36 @@
                 barrier, inc=1, device_id=device(member, place), device_id_type=MESH
             )
 
-    def lanes_of(target, tile):
-        start = (lax.rem(target, pair) * tiles + tile) * LANES
-        return x_hbm.at[:, :, :, pl.ds(pl.multiple_of(start, LANES), LANES)]
-
-    own_tiles = [
-        pltpu.make_async_copy(lanes_of(me, tile), raw.at[me, tile], load_sem.at[2 + tile])
-        for tile in range(tiles)
+    loads = [
+        pltpu.make_async_copy(
+            x_hbm.at[:, :, :, lane * LANES : (lane + 1) * LANES], own.at[lane], load_sem.at[2 + lane]
+        )
+        for lane in range(pair * tiles)
     ]
     load_bins = pltpu.make_async_copy(bins_hbm, bins_all.at[me], load_sem.at[0])
     load_table = pltpu.make_async_copy(
         table_hbm.at[lax.axis_index("sub"), pl.ds(side * tiles, tiles)], table, load_sem.at[1]
     )
     load_bins.start()
-    for own_tile in own_tiles:
-        own_tile.start()
+    for load in loads:
+        load.start()
     load_table.start()
 
+    load_bins.wait()
+    for load in loads:
+        load.wait()
     pl.semaphore_wait(barrier, chans - 1 + pair * (spots - 1))
 
     def bins_copy(source, target):
         return pltpu.make_async_remote_copy(
-            src_ref=bins_hbm, dst_ref=bins_all.at[source],
+            src_ref=bins_all.at[me], dst_ref=bins_all.at[source],
             send_sem=bins_send.at[target], recv_sem=bins_recv.at[source],
             device_id={"chan": target}, device_id_type=MESH,
         )
 
     def block_copy(source, target, tile):
         return pltpu.make_async_remote_copy(
-            src_ref=lanes_of(target, tile), dst_ref=raw.at[source, tile],
+            src_ref=own.at[lax.rem(target, pair) * tiles + tile], dst_ref=raw.at[source, tile],
             send_sem=block_send.at[target, tile], recv_sem=block_recv.at[source, tile],
             device_id={"chan": target}, device_id_type=MESH,
         )
@@ -102,7 +106,8 @@
         for target in others:
             block_copy(me, target, tile).start()
 
-    load_bins.wait()
+    for tile in range(tiles):
+        raw[me, tile] = own[side * tiles + tile]
     for source in others:
         bins_copy(source, source).wait_recv()
     padded = weights.shape[2]
@@ -126,7 +131,6 @@
     rows = seg_dev * 2 * ch
 
     for tile in range(tiles):
-        own_tiles[tile].wait()
         for source in others:
             block_copy(source, me, tile).wait_recv()
 
@@ -164,10 +168,13 @@
             zero = jnp.zeros((ch, LANES), jnp.float32)
             diag_re, diag_im = lax.fori_loop(0, chans, mix, (zero, zero), unroll=unroll)
 
-            def rows_of(group, carry, diag_re=diag_re, diag_im=diag_im):
-                first = group * out_rows
-
-                def add(a, sums):
+            last = tile == tiles - 1
+            if tile == 0 and step == 0:
+                load_table.wait()
+            for place in near + [spot]:
+                first = place * out_rows
+
+                def add(a, sums, first=first):
                     sums = list(sums)
                     for k in range(seg_dev):
                         re, im = k * 2 * ch, (k * 2 + 1) * ch
@@ -181,43 +188,41 @@
 
                 start = tuple(jnp.zeros((ch, LANES), jnp.float32) for _ in range(2 * out_rows))
                 sums = lax.fori_loop(0, chans, add, start, unroll=unroll)
+                pieces = []
                 for r in range(out_rows):
                     diag = j_ids == first + r
-                    at = pl.ds(pl.multiple_of((first + r) * ch, ch), ch)
-                    cross[at, :LANES] = jnp.where(diag, diag_re, sums[2 * r]).astype(jnp.bfloat16)
-                    cross[at, LANES:] = jnp.where(diag, diag_im, sums[2 * r + 1]).astype(
-                        jnp.bfloat16
+                    pieces.append(
+                        jnp.concatenate(
+                            [
+                                jnp.where(diag, diag_re, sums[2 * r]).astype(jnp.bfloat16),
+                                jnp.where(diag, diag_im, sums[2 * r + 1]).astype(jnp.bfloat16),
+                            ],
+                            axis=1,
+                        )
                     )
-                return carry
-
-            lax.fori_loop(0, spots, rows_of, 0)
-            if tile == 0 and step == 0:
-                load_table.wait()
-            lags = jnp.dot(cross[...], table[tile], preferred_element_type=jnp.float32)
-            if tile > 0:
-                lags = lags + total[member]
-            if tile < tiles - 1:
-                total[member] = lags
-                continue
-            lags = lags * norm
-            for place in range(spots):
-                leave[member, place] = lags[place * depth : (place + 1) * depth].astype(jnp.bfloat16)
-            if step < pair - 1:
-                part_copy(member, spot, side, spot).start()
-            else:
-                total[member] = lags
-            for place in near:
-                part_copy(member, place, side, spot).start()
-
-    own = total[side, pl.ds(pl.multiple_of(spot * depth, depth), depth), :]
+                cross = jnp.concatenate(pieces, axis=0)
+                lags = jnp.dot(cross, table[tile], preferred_element_type=jnp.float32)
+                if tile > 0:
+                    lags = lags + total[member, place]
+                if not last:
+                    total[member, place] = lags
+                    continue
+                lags = lags * norm
+                if step == pair - 1 and place is spot:
+                    total[side, spot] = lags
+                else:
+                    leave[member, place] = lags.astype(jnp.bfloat16)
+                    part_copy(member, place, side, spot).start()
+
+    result = total[side, spot]
     for step in range(pair):
         member = lax.rem(side + 1 + step, pair)
         for place in near + [spot] * (step < pair - 1):
             part_copy(member, place, member, place).wait_recv()
-            own = own + land[member, place].astype(jnp.float32)
-    own = own * scale
+            result = result + land[member, place].astype(jnp.float32)
+    result = result * scale
     for r in range(out_rows):
-        out_ref[0, r] = own[r * ch : (r + 1) * ch].astype(jnp.bfloat16)
+        out_ref[0, r] = result[r * ch : (r + 1) * ch].astype(jnp.bfloat16)
 
     for target in others:
         bins_copy(me, target).wait_send()
@@ -248,14 +253,14 @@
         in_specs=[in_hbm, in_hbm, in_hbm],
         out_specs=pl.BlockSpec(memory_space=pltpu.VMEM),
         scratch_shapes=[
+            pltpu.VMEM((pair * tiles, seg_dev, ch, 2, LANES), jnp.bfloat16),
             pltpu.VMEM((chans, tiles, seg_dev, ch, 2, LANES), jnp.bfloat16),
             pltpu.VMEM((chans, 1, chans), jnp.int32),
             pltpu.VMEM((tiles, 2 * LANES, LAGS), jnp.bfloat16),
             pltpu.VMEM((chans, rows, LANES), jnp.float32),
             pltpu.VMEM((chans, rows, LANES), jnp.float32),
             pltpu.VMEM((pair, chans, padded, LANES), jnp.float32),
-            pltpu.VMEM((ch * ch, 2 * LANES), jnp.bfloat16),
-            pltpu.VMEM((pair, ch * ch, LAGS), jnp.float32),
+            pltpu.VMEM((pair, spots, out_rows * ch, LAGS), jnp.float32),
             pltpu.VMEM((pair, spots, out_rows * ch, LAGS), jnp.bfloat16),
             pltpu.VMEM((pair, spots, out_rows * ch, LAGS), jnp.bfloat16),
             dma((chans,)),
@@ -264,7 +269,7 @@
             dma((chans, tiles)),
             dma((pair, spots)),
             dma((pair, spots)),
-            dma((2 + tiles,)),
+            dma((2 + pair * tiles,)),
         ],
         compiler_params=pltpu.CompilerParams(
             collective_id=0, has_side_effects=True, vmem_limit_bytes=60 * 2**20

time: 16 us -> 15.4 us (0.963)
  Pallas kernels: 15.2 us -> 14.7 us
    pallas_call x1, Pallas kernels: 15.2 us -> 14.7 us  [local(): pl.pallas_call(functools.partial(kernel, sizes), out_shape=pltpu.VMEM((1,...]
where the time goes in v3:
time: 15.4 us; the launch traced here: 15.3 us
  Pallas kernels  14.7 us (95%)
  local copies, waits for them, and re-layouts  0.61 us (4%)
    pallas_call x1, Pallas kernels, local(): pl.pallas_call(functools.partial(kernel, sizes), out_shape=pltpu.VMEM((1,...  14.7 us
    unnamed x1, local copies, waits for them, and re-layouts  0.61 us

profile of v3, /device:TPU:0, one launch (start us, length us, event | category | flops | bytes accessed | tf_op | source)
XLA Modules:
  0.0 15.3 jit_solution(16348079893952835530)
XLA Ops:
  0.0 14.7 %shard_map.37 = bf16[1,4,16,128]{3,2,1,0:T(8,128)(2,1)S(1)} custom-call(bf16[2,16,2,512]{3,2,1,0:T(2,128)(2,1)} %x_hbm.1, s32[1,4]{1,0:T(1,128)} %bins_hbm.1, bf16[2,4,256,128]{3,2,1,0:T(8,128)(2,1)} %constant.2.clone.table_hbm), custom_call_target="tpu_custom_call" | custom-call | tf_op jit(solution)/shard_map/pallas_call | solution.py:250
  14.7 0.6 %copy.5 = bf16[1,4,16,128]{3,2,1,0:T(8,128)(2,1)} copy(bf16[1,4,16,128]{3,2,1,0:T(8,128)(2,1)S(1)} %shard_map.37) | data formatting | bytes 32768

commit v4 on v3

--- a/solution.py
+++ b/solution.py
@@ -171,7 +171,8 @@
             last = tile == tiles - 1
             if tile == 0 and step == 0:
                 load_table.wait()
-            for place in near + [spot]:
+            crosses = []
+            for turn, place in enumerate(near + [spot]):
                 first = place * out_rows
 
                 def add(a, sums, first=first):
@@ -201,20 +202,24 @@
                         )
                     )
                 cross = jnp.concatenate(pieces, axis=0)
+                if not last:
+                    crosses.append(cross)
+                    continue
                 lags = jnp.dot(cross, table[tile], preferred_element_type=jnp.float32)
                 if tile > 0:
-                    lags = lags + total[member, place]
-                if not last:
-                    total[member, place] = lags
-                    continue
+                    lags = lags + total[step, turn]
                 lags = lags * norm
                 if step == pair - 1 and place is spot:
-                    total[side, spot] = lags
+                    result = lags
                 else:
                     leave[member, place] = lags.astype(jnp.bfloat16)
                     part_copy(member, place, side, spot).start()
-
-    result = total[side, spot]
+            if not last:
+                lags = jnp.dot(
+                    jnp.concatenate(crosses, axis=0), table[tile], preferred_element_type=jnp.float32
+                ).reshape(total.shape[1:])
+                total[step] = lags if tile == 0 else lags + total[step]
+
     for step in range(pair):
         member = lax.rem(side + 1 + step, pair)
         for place in near + [spot] * (step < pair - 1):

time: 15.4 us -> 15.4 us (level)
  no operation moved by 1% of the time
where the time goes in v4:
time: 15.4 us; the launch traced here: 15.3 us
  Pallas kernels  14.7 us (95%)
  local copies, waits for them, and re-layouts  0.61 us (4%)
    pallas_call x1, Pallas kernels, local(): pl.pallas_call(functools.partial(kernel, sizes), out_shape=pltpu.VMEM((1,...  14.7 us
    unnamed x1, local copies, waits for them, and re-layouts  0.61 us

profile of v4, /device:TPU:0, one launch (start us, length us, event | category | flops | bytes accessed | tf_op | source)
XLA Modules:
  0.0 15.3 jit_solution(16621376877777719671)
XLA Ops:
  0.0 14.7 %shard_map.37 = bf16[1,4,16,128]{3,2,1,0:T(8,128)(2,1)S(1)} custom-call(bf16[2,16,2,512]{3,2,1,0:T(2,128)(2,1)} %x_hbm.1, s32[1,4]{1,0:T(1,128)} %bins_hbm.1, bf16[2,4,256,128]{3,2,1,0:T(8,128)(2,1)} %constant.2.clone.table_hbm), custom_call_target="tpu_custom_call" | custom-call | tf_op jit(solution)/shard_map/pallas_call | solution.py:255
  14.7 0.6 %copy.5 = bf16[1,4,16,128]{3,2,1,0:T(8,128)(2,1)} copy(bf16[1,4,16,128]{3,2,1,0:T(8,128)(2,1)S(1)} %shard_map.37) | data formatting | bytes 32768
